TPU v7x, 1024 devices: a whole 8x8x8 slice. The times are simulated.
1024 devices in a mesh: ctx: 64 (over z, x), head: 16 (over y, core).
Axes of the slice: x: 8, y: 8, z: 8, core: 2. Of those that a mesh axis runs over, the one named last changes fastest.
Arguments:
- query_nope: bfloat16 [256, 16384], P('head'), may hold values from -6 to 6
- query_rope: bfloat16 [256, 8192], P('head'), may hold values from -10 to 10
- latent_cache: bfloat16 [32768, 512], P('ctx'), may hold values from -6 to 6
- rope_keys: bfloat16 [64, 32768], P(None, 'ctx'), may hold values from -6 to 6
- absorb_keys: bfloat16 [128, 128, 512], P('head'), may hold values from -0.5 to 0.5
- expand_values: bfloat16 [128, 512, 128], P('head'), may hold values from -2.09375 to 2.09375
- block_ids: int32 [128, 2, 16], P('head'), may hold values from -1 to 255, as said below
- block_counts: int32 [128, 2], P('head'), may hold values from 8 to 16
Outputs:
- attended: bfloat16 [256, 16384], P('head')
Inputs may be any that keep to these rules, and one draw needn't show every extreme that they name: `block_ids`: entries beyond block_counts are -1; the first block_counts entries are distinct blocks, none after the query block's own block 254 + q, and entry 0 is that own block.
All inputs are finite; a program needn't handle non-finite values.
Results may differ from a plain program's by a relative error of at most 0.0066.
Values may be sent and summed in bfloat16 or wider, within the bound.
A program may use at most 32 MiB of HBM per device.

v0:
```python
import math

import jax
import jax.numpy as jnp
from jax import lax
from jax.sharding import PartitionSpec as P

BLOCK = 128


def body(
    query_nope,
    query_rope,
    latent_cache,
    rope_keys,
    absorb_keys,
    expand_values,
    block_ids,
    block_counts,
):
    nope_all, rope_all = (
        lax.all_to_all(query_nope, "head", split_axis=1, concat_axis=0, tiled=True),
        lax.all_to_all(query_rope, "head", split_axis=1, concat_axis=0, tiled=True),
    )
    tokens = nope_all.shape[0]
    heads_here = absorb_keys.shape[0]
    nope_width = absorb_keys.shape[1]
    rope_width = rope_keys.shape[0]
    value_width = expand_values.shape[2]
    keys_here = latent_cache.shape[0]
    blocks_here = keys_here // BLOCK
    query_blocks = tokens // BLOCK
    slot_count = block_ids.shape[2]
    shards = lax.axis_size("ctx")
    ctx_index = lax.axis_index("ctx")
    score_scale = 1.0 / math.sqrt(nope_width + rope_width)
    query_latent = jnp.einsum(
        "thn,hnl->htl",
        nope_all.reshape(tokens, heads_here, nope_width),
        absorb_keys,
        preferred_element_type=jnp.float32,
    ).astype(jnp.bfloat16)
    scores = jnp.einsum(
        "htl,kl->htk", query_latent, latent_cache, preferred_element_type=jnp.float32
    )
    scores = scores + jnp.einsum(
        "thr,rk->htk",
        rope_all.reshape(tokens, heads_here, rope_width),
        rope_keys,
        preferred_element_type=jnp.float32,
    )
    scores = (scores * score_scale).reshape(heads_here, query_blocks, BLOCK, blocks_here, BLOCK)
    block_global = ctx_index * blocks_here + jnp.arange(blocks_here, dtype=jnp.int32)
    slot_live = jnp.arange(slot_count, dtype=jnp.int32)[None, None, :] < block_counts[:, :, None]
    chosen = jnp.any((block_ids[..., None] == block_global) & slot_live[..., None], axis=2)
    query_pos = keys_here * shards - tokens + jnp.arange(tokens, dtype=jnp.int32)
    key_pos = ctx_index * keys_here + jnp.arange(keys_here, dtype=jnp.int32)
    causal = (key_pos[None, :] <= query_pos[:, None]).reshape(
        query_blocks, BLOCK, blocks_here, BLOCK
    )
    allowed = chosen[:, :, None, :, None] & causal[None]
    local_top = jnp.max(jnp.where(allowed, scores, -1e30), axis=(3, 4))
    weights = jnp.where(allowed, jnp.exp(scores - local_top[..., None, None]), 0.0).astype(
        jnp.bfloat16
    )
    weights = weights.reshape(heads_here, tokens, keys_here)
    top_rows = local_top.reshape(heads_here, tokens).T
    weight_total = jnp.sum(weights, axis=2, dtype=jnp.float32).T
    latent_sum = jnp.einsum(
        "htk,kl->thl", weights, latent_cache, preferred_element_type=jnp.float32
    )
    value_float = expand_values.astype(jnp.float32)
    per_device = tokens // shards
    row_top = lax.pmax(top_rows, "ctx")
    factor = jnp.exp(top_rows - row_top)
    owned_sum, owned_total = (
        lax.psum_scatter(latent_sum * factor[..., None], "ctx", scatter_dimension=0, tiled=True),
        lax.psum_scatter(weight_total * factor, "ctx", scatter_dimension=0, tiled=True),
    )
    expanded = (
        jnp.einsum("thl,hlv->thv", owned_sum, value_float, precision=lax.Precision.HIGHEST)
        / owned_total[..., None]
    )
    rows_done = expanded.astype(jnp.bfloat16).reshape(per_device, heads_here * value_width)
    merged = lax.all_gather(rows_done, "ctx", axis=0, tiled=True)
    return lax.all_to_all(merged, "head", split_axis=0, concat_axis=1, tiled=True)


def solution(mesh):
    return jax.shard_map(
        body,
        mesh=mesh,
        in_specs=(
            P("head", None),
            P("head", None),
            P("ctx", None),
            P(None, "ctx"),
            P("head", None, None),
            P("head", None, None),
            P("head", None, None),
            P("head", None),
        ),
        out_specs=P("head", None),
        check_vma=False,
    )
```

profile of v0, /device:TPU:1, one launch (start us, length us, event | category | flops | bytes accessed | tf_op | source)
XLA Modules:
  0.0 551.0 jit_solution(3136301649373858204)
XLA Ops:
  6.5 1.8 copy.62
  8.3 17.5 %all-to-all-start.1 = ((bf16[16,16,512]{2,0,1:T(8,128)(2,1)}), bf16[16,16,512]{2,0,1:T(8,128)(2,1)S(1)}, u32[]{:S(2)}, u32[]{:S(2)}) async-start(bf16[16,16,512]{2,0,1:T(8,128)(2,1)} %bitcast.55), calls=%async_computation.1 | async-start | bytes 524288 | tf_op jit(solution)/shard_map/all_to_all | solution.py:23
  25.8 1.9 copy.61
  27.6 10.0 %all-to-all-done.1 = bf16[16,16,512]{2,0,1:T(8,128)(2,1)S(1)} async-done(((bf16[16,16,512]{2,0,1:T(8,128)(2,1)}), bf16[16,16,512]{2,0,1:T(8,128)(2,1)S(1)}, u32[]{:S(2)}, u32[]{:S(2)}) %all-to-all-start.1) | async-done | bytes 262176 | tf_op jit(solution)/shard_map/all_to_all | solution.py:23
  37.6 4.1 all-to-all-start
  41.8 0.0 reduce-scatter.3.cloned.1.call-start
  41.8 0.7 copy.33
  42.5 0.8 iota_compare_fusion
  43.3 0.3 and_reduce_fusion
  43.6 0.1 copy.34
  43.7 0.6 and.28
  44.3 2.3 and.29
  46.7 0.1 broadcast_compare_fusion
  46.8 0.3 reshape.85
  47.1 11.2 %all-to-all-done = bf16[16,16,1024]{2,0,1:T(8,128)(2,1)} async-done(((bf16[16,16,1024]{2,0,1:T(8,128)(2,1)}), bf16[16,16,1024]{2,0,1:T(8,128)(2,1)}, u32[]{:S(2)}, u32[]{:S(2)}) %all-to-all-start) | async-done | bytes 524320 | tf_op jit(solution)/shard_map/all_to_all | solution.py:22
  58.4 1.1 copy.49
  59.5 4.7 fusion.1
  64.3 3.5 select_reduce_fusion
  67.7 1.9 copy-done.1
  69.7 1.7 convert_reduce_fusion
  71.4 122.2 %pmax.7 = f32[256,8]{0,1:T(8,128)S(1)} all-reduce(f32[256,8]{0,1:T(8,128)S(1)} %bitcast.61), channel_id=1, replica_groups=mesh['ctx'=64,'head'=16] {'ctx'}, use_global_device_ids=true, to_apply=%region_2.3 | all-reduce | flops 2048 | bytes 16384 | tf_op jit(solution)/shard_map/pmax | solution.py:74
  193.6 3.2 bitcast_multiply_fusion
  196.8 4.4 copy.40
  201.2 1.4 dynamic-slice
  203.2 113.1 %all-reduce = f32[256,8]{0,1:T(8,128)S(1)} all-reduce(f32[256,8]{0,1:T(8,128)S(1)} %get-tuple-element.5), channel_id=3, replica_groups=mesh['ctx'=64,'head'=16] {'ctx'}, use_global_device_ids=true, to_apply=%region_5.6.clone | all-reduce | flops 2048 | bytes 16384
  316.3 0.1 constant_dynamic-slice_fusion
  316.4 148.1 %reduce-scatter.3.cloned.1.call-done = f32[4,8,512]{2,1,0:T(8,128)} async-done(((f32[256,8,512]{2,1,0:T(8,128)}), f32[4,8,512]{2,1,0:T(8,128)}) %reduce-scatter.3.cloned.1.call-update) | async-done | bytes 65552 | tf_op jit(solution)/shard_map/reduce_scatter | solution.py:77
  464.5 1.4 fusion.7
  465.9 35.9 %all-gather = bf16[64,4,1024]{2,1,0:T(4,128)(2,1)S(1)} all-gather(bf16[1,4,1024]{2,1,0:T(4,128)(2,1)S(1)} %fusion.7), channel_id=1, replica_groups=mesh['ctx'=64,'head'=16] {'ctx'}, dimensions={0}, use_global_device_ids=true | all-gather | bytes 532480 | tf_op jit(solution)/shard_map/all_gather | solution.py:85
  501.8 0.1 all_to_all.44
  501.9 41.5 %all_to_all.51 = bf16[16,16,1024]{2,1,0:T(8,128)(2,1)S(1)} all-to-all(bf16[16,16,1024]{2,1,0:T(8,128)(2,1)S(1)} %all_to_all.44), channel_id=1, replica_groups=mesh['ctx'=64,'head'=16] {'head'}, dimensions={0} | all-to-all | bytes 1048576 | tf_op jit(solution)/shard_map/all_to_all | solution.py:86
  543.4 0.8 copy.48
  (14 shorter events, 0.1 us)
Async XLA Ops:
  6.5 53.0 %copy-start = (bf16[8,128,512]{2,1,0:T(8,128)(2,1)S(1)}, bf16[8,128,512]{2,1,0:T(8,128)(2,1)}, u32[]{:S(2)}) copy-start(bf16[8,128,512]{2,1,0:T(8,128)(2,1)} %param.12) | copy-start | bytes 3145732
  8.3 29.3 %all-to-all-start.1 = ((bf16[16,16,512]{2,0,1:T(8,128)(2,1)}), bf16[16,16,512]{2,0,1:T(8,128)(2,1)S(1)}, u32[]{:S(2)}, u32[]{:S(2)}) async-start(bf16[16,16,512]{2,0,1:T(8,128)(2,1)} %bitcast.55), calls=%async_computation.1 | async-start | bytes 524288 | tf_op jit(solution)/shard_map/all_to_all | solution.py:23
  37.6 20.7 %all-to-all-start = ((bf16[16,16,1024]{2,0,1:T(8,128)(2,1)}), bf16[16,16,1024]{2,0,1:T(8,128)(2,1)}, u32[]{:S(2)}, u32[]{:S(2)}) async-start(bf16[16,16,1024]{2,0,1:T(8,128)(2,1)} %bitcast.54), calls=%async_computation | async-start | bytes 1048576 | tf_op jit(solution)/shard_map/all_to_all | solution.py:22
  41.8 422.7 %reduce-scatter.3.cloned.1.call-start = ((), (), s32[]{:S(2)}) async-start(), calls=%async_computation.4 | async-start | bytes 4259840 | tf_op jit(solution)/shard_map/reduce_scatter | solution.py:77
  46.7 17.6 %copy-start.4 = (bf16[64,512]{1,0:T(8,128)(2,1)S(1)}, bf16[64,512]{1,0:T(8,128)(2,1)}, u32[]{:S(2)}) copy-start(bf16[64,512]{1,0:T(8,128)(2,1)} %param.11) | copy-start | bytes 196612
  67.7 1.9 copy-start.1
  67.7 125.8 %copy-start.2 = (bf16[512,512]{1,0:T(8,128)(2,1)S(1)}, bf16[512,512]{1,0:T(8,128)(2,1)}, u32[]{:S(2)}) copy-start(bf16[512,512]{1,0:T(8,128)(2,1)} %param.10) | copy-start | bytes 1572868
  201.2 263.3 %copy-start.3 = (bf16[8,512,128]{2,1,0:T(8,128)(2,1)S(1)}, bf16[8,512,128]{2,1,0:T(8,128)(2,1)}, u32[]{:S(2)}) copy-start(bf16[8,512,128]{2,1,0:T(8,128)(2,1)} %param.13) | copy-start | bytes 3145732
Sparse Core Ops, SparseCore 0:
  201.3 263.1 reduce-scatter.2
where the time goes:
time: 552 us; the launch traced here: 551 us
  blocking collectives  313 us (57%)
  waiting for transfers between devices  169 us (31%)
  starting transfers between devices  21.7 us (4%)
  local copies, waits for them, and re-layouts  17.5 us (3%)
  between operations  14.2 us (3%)
  matrix products  12.8 us (2%)
    reduce_scatter x1, waiting for transfers between devices, body(): lax.psum_scatter(latent_sum * factor[..., None], 'ctx', scatter_dimension...  148 us
    pmax x1, blocking collectives, body(): row_top = lax.pmax(top_rows, 'ctx')  122 us
    unnamed x1, blocking collectives  113 us
    all_to_all x1, blocking collectives, body(): lax.all_to_all(merged, 'head', split_axis=0, concat_axis=1, tiled=True)  41.5 us
    all_gather x1, blocking collectives, body(): merged = lax.all_gather(rows_done, 'ctx', axis=0, tiled=True)  35.9 us
    all_to_all x1, starting transfers between devices, body(): lax.all_to_all(query_rope, 'head', split_axis=1, concat_axis=0, tiled=True)  17.5 us
    all_to_all x1, waiting for transfers between devices, body(): lax.all_to_all(query_nope, 'head', split_axis=1, concat_axis=0, tiled=True)  11.2 us
  transfers between devices with their start and end apart: 3, of which 3 were waited for; matrix products, arithmetic and copies ran while one was open for 2% of the time, Pallas kernels for 0%

commit v1 on v0

v1 whole, which is shorter than its diff:
```python
import functools
import math

import jax
import jax.numpy as jnp
from jax import lax
from jax.experimental import pallas as pl
from jax.experimental.pallas import tpu as pltpu
from jax.sharding import PartitionSpec as P

BLOCK = 128
MESH = pl.DeviceIdType.MESH
NONE = -1e30
F32 = jnp.float32
BF16 = jnp.bfloat16


def ring_order(n):
    order = []
    for d in range(1, n // 2 + 1):
        order.append(d)
        if n - d not in order:
            order.append(n - d)
    return order


def wait_bytes(ref, sem):
    pltpu.make_async_copy(ref, ref, sem).wait()


def kernel(
    n,
    qn_hbm,
    qr_hbm,
    lat_hbm,
    rk_hbm,
    ak_hbm,
    ev_hbm,
    ids_ref,
    counts_ref,
    out_ref,
    qn,
    qr,
    lat,
    rk,
    ak,
    ev,
    rkpad,
    vext,
    bias,
    q_send,
    q_recv,
    o1_send,
    l1_send,
    o1_recv,
    l1_recv,
    o2_send,
    l2_send,
    o2_recv,
    l2_recv,
    done,
    rows_all,
    load_sem,
    qs_sem,
    qr_sem,
    s1_sem,
    r1_sem,
    s2_sem,
    r2_sem,
    s3_sem,
    r3_sem,
    s4_sem,
    r4_sem,
):
    c = lax.axis_index("ctx")
    g = lax.axis_index("head")
    z, x = c // n, lax.rem(c, n)
    y, core = g // 2, lax.rem(g, 2)
    tok = qn.shape[0]
    half = n * tok
    nope = ak.shape[1]
    rope = rk.shape[0]
    keys = lat.shape[0]
    slots = ids_ref.shape[2]
    vdim = ev.shape[2]
    pairs = n // 2
    wn, wr = 2 * nope, 2 * rope
    ring = ring_order(n)

    loads = [
        pltpu.make_async_copy(src, dst, load_sem.at[i])
        for i, (src, dst) in enumerate(
            (
                (qn_hbm, qn),
                (qr_hbm, qr),
                (lat_hbm, lat),
                (ev_hbm, ev),
                (rk_hbm, rk),
                (ak_hbm, ak),
            )
        )
    ]
    for copy in loads:
        copy.start()

    def at(pos, d):
        return lax.rem(pos + d, n)

    y_peers = [(0, 1)] + [(d, dc) for d in ring for dc in (0, 1)]
    barrier = pltpu.get_barrier_semaphore()
    for d, dc in y_peers:
        peer = 2 * at(y, d) + lax.rem(core + dc, 2)
        pl.semaphore_signal(barrier, inc=1, device_id=(c, peer), device_id_type=MESH)
    for d in ring:
        pl.semaphore_signal(barrier, inc=1, device_id=(z * n + at(x, d), g), device_id_type=MESH)
        pl.semaphore_signal(barrier, inc=1, device_id=(at(z, d) * n + x, g), device_id_type=MESH)

    loads[0].wait()
    loads[1].wait()
    for to in range(2 * n):
        for p in range(pairs):
            at_n = (to * pairs + p) * wn
            at_r = (to * pairs + p) * wr
            q_send[p, to, :, 0:wn] = qn[:, at_n : at_n + wn]
            q_send[p, to, :, wn : wn + wr] = qr[:, at_r : at_r + wr]
    first = lax.rem(x + z, n) // 2
    my_rows = pl.multiple_of(core * half + y * tok, tok)

    pl.semaphore_wait(barrier, len(y_peers) + 2 * len(ring))

    def send_pair(i, carry):
        p = lax.rem(first + i, pairs)
        for d, dc in y_peers:
            peer = 2 * at(y, d) + lax.rem(core + dc, 2)
            pltpu.make_async_remote_copy(
                src_ref=q_send.at[p, peer],
                dst_ref=q_recv.at[p, pl.ds(my_rows, tok)],
                send_sem=qs_sem,
                recv_sem=qr_sem.at[p],
                device_id=(c, peer),
                device_id_type=MESH,
            ).start()
        return carry

    lax.fori_loop(0, pairs, send_pair, 0)
    for p in range(pairs):
        q_recv[p, pl.ds(my_rows, tok)] = q_send[p, g]

    lane = lax.broadcasted_iota(jnp.int32, (1, slots), 1)
    for h in range(n):
        for q in range(2):
            ids = ids_ref[h, q : q + 1, :]
            live = lane < counts_ref[q, h]
            for b in range(keys // BLOCK):
                hit = (ids == c * (keys // BLOCK) + b) & live
                chosen = jnp.max(jnp.where(hit, 0.0, NONE), axis=1, keepdims=True)
                bias[h, q : q + 1, b * BLOCK : (b + 1) * BLOCK] = jnp.broadcast_to(chosen, (1, BLOCK))

    loads[4].wait()
    rkpad[...] = jnp.zeros_like(rkpad)
    rkpad[0, 0:rope] = rk[...]
    rkpad[1, rope : 2 * rope] = rk[...]
    loads[2].wait()
    loads[3].wait()
    vext[:, :, vdim:] = jnp.ones((n, keys, vext.shape[2] - vdim), BF16)

    def make_values(h, carry):
        vext[h, :, 0:vdim] = jnp.dot(lat[...], ev[h], preferred_element_type=F32).astype(BF16)
        return carry

    lax.fori_loop(0, n, make_values, 0)
    loads[5].wait()

    scale = 1.0 / math.sqrt(nope + rope)
    row = lax.broadcasted_iota(jnp.int32, (2 * half, 1), 0)
    in_half = lax.rem(row, half)
    token = (2 * (in_half // tok) + row // half) * tok + lax.rem(in_half, tok)
    context = keys * n * n
    query_pos = context - 2 * half + token
    late = keys // 2
    key_pos = c * keys + late + lax.broadcasted_iota(jnp.int32, (1, keys - late), 1)

    def attend(i, carry):
        p = lax.rem(first + i, pairs)
        wait_bytes(q_recv.at[p, pl.ds(0, 2 * half - tok)], qr_sem.at[p])
        for k in range(2):
            h = 2 * p + k
            query_latent = jnp.dot(
                q_recv[p, :, k * nope : (k + 1) * nope], ak[h], preferred_element_type=F32
            ).astype(BF16)
            scores = lax.dot_general(
                query_latent, lat[...], (((1,), (1,)), ((), ())), preferred_element_type=F32
            )
            scores = scores + jnp.dot(
                q_recv[p, :, wn : wn + wr], rkpad[k], preferred_element_type=F32
            )
            scores = scores * scale
            low, high = bias[h, 0:1], bias[h, 1:2]
            quarter = (half // 2, keys)
            mask = jnp.concatenate(
                [jnp.broadcast_to(v, quarter) for v in (low, high, low, high)], axis=0
            )
            scores = scores + mask
            scores = jnp.concatenate(
                [
                    scores[:, :late],
                    jnp.where(key_pos <= query_pos, scores[:, late:], NONE),
                ],
                axis=1,
            )
            top = jnp.max(scores, axis=1, keepdims=True)
            weights = jnp.exp(scores - top).astype(BF16)
            summed = jnp.dot(weights, vext[h], preferred_element_type=F32)
            total = summed[:, vdim : 2 * vdim]
            mixed = summed[:, :vdim] / total
            level = top + jnp.log(total)
            for e in range(2):
                part = slice(e * half, (e + 1) * half)
                o1_send[e, h] = mixed[part].astype(BF16)
                l1_send[e, h] = jnp.transpose(level[part, 0:BLOCK])[0:8]
                mine = x if e == 0 else z
                to = z * n + h if e == 0 else h * n + x
                slot = lax.rem(h - mine + n, n) - 1

                @pl.when(h != mine)
                def _(e=e, h=h, to=to, slot=slot):
                    pltpu.make_async_remote_copy(
                        src_ref=o1_send.at[e, h],
                        dst_ref=o1_recv.at[e, slot],
                        send_sem=s1_sem.at[e, 0],
                        recv_sem=r1_sem.at[e, 0],
                        device_id=(to, g),
                        device_id_type=MESH,
                    ).start()
                    pltpu.make_async_remote_copy(
                        src_ref=l1_send.at[e, h],
                        dst_ref=l1_recv.at[e, slot],
                        send_sem=s1_sem.at[e, 1],
                        recv_sem=r1_sem.at[e, 1],
                        device_id=(to, g),
                        device_id_type=MESH,
                    ).start()

        return carry

    lax.fori_loop(0, pairs, attend, 0)

    for e in range(2):
        mine = x if e == 0 else z
        wait_bytes(o1_recv.at[e], r1_sem.at[e, 0])
        wait_bytes(l1_recv.at[e], r1_sem.at[e, 1])
        levels = jnp.concatenate(
            [l1_send[e, mine][0:1]] + [l1_recv[e, k][0:1] for k in range(n - 1)], axis=0
        )
        top = jnp.max(levels, axis=0, keepdims=True)
        share = jnp.exp(levels - top)
        whole = jnp.sum(share, axis=0, keepdims=True)
        table = jnp.concatenate(
            [share / whole, jnp.broadcast_to(top + jnp.log(whole), (n, half))], axis=0
        )
        columns = jnp.transpose(table)
        mixed = columns[:, 0:1] * o1_send[e, mine].astype(F32)
        for k in range(n - 1):
            mixed = mixed + columns[:, k + 1 : k + 2] * o1_recv[e, k].astype(F32)
        o2_send[e] = mixed.astype(BF16)
        l2_send[e] = jnp.broadcast_to(columns[:, n : n + 1], (half, BLOCK))
        for d in ring:
            other = at(z, d) if e == 0 else at(x, d)
            to = other * n + x if e == 0 else z * n + other
            rows = pl.ds(pl.multiple_of(other * tok, tok), tok)
            pltpu.make_async_remote_copy(
                src_ref=o2_send.at[e, rows],
                dst_ref=o2_recv.at[e, d - 1],
                send_sem=s2_sem.at[e, 0],
                recv_sem=r2_sem.at[e, 0],
                device_id=(to, g),
                device_id_type=MESH,
            ).start()
            pltpu.make_async_remote_copy(
                src_ref=l2_send.at[e, rows],
                dst_ref=l2_recv.at[e, d - 1],
                send_sem=s2_sem.at[e, 1],
                recv_sem=r2_sem.at[e, 1],
                device_id=(to, g),
                device_id_type=MESH,
            ).start()

    selves = []
    for e in range(2):
        pos = z if e == 0 else x
        wait_bytes(o2_recv.at[e], r2_sem.at[e, 0])
        wait_bytes(l2_recv.at[e], r2_sem.at[e, 1])
        rows = pl.ds(pl.multiple_of(pos * tok, tok), tok)
        levels = [l2_send[e, rows]] + [l2_recv[e, k] for k in range(n - 1)]
        top = functools.reduce(jnp.maximum, levels)
        shares = [jnp.exp(level - top) for level in levels]
        mixed = shares[0] * o2_send[e, rows].astype(F32)
        whole = shares[0]
        for k in range(n - 1):
            mixed = mixed + shares[k + 1] * o2_recv[e, k].astype(F32)
            whole = whole + shares[k + 1]
        done[e] = (mixed / whole).astype(BF16)
        place = x if e == 0 else z
        peer = 2 * pos + e
        is_self = g == peer
        selves.append(is_self)
        for d in ring:
            to = at(z, d) * n + x if e == 0 else z * n + at(x, d)
            pltpu.make_async_remote_copy(
                src_ref=done.at[e],
                dst_ref=rows_all.at[place, g],
                send_sem=s3_sem.at[e],
                recv_sem=r3_sem,
                device_id=(to, peer),
                device_id_type=MESH,
            ).start()

        @pl.when(is_self)
        def _(e=e, place=place):
            pltpu.make_async_copy(done.at[e], rows_all.at[place, g], r3_sem).start()

        @pl.when(jnp.logical_not(is_self))
        def _(e=e, place=place, peer=peer):
            pltpu.make_async_remote_copy(
                src_ref=done.at[e],
                dst_ref=rows_all.at[place, g],
                send_sem=s3_sem.at[e],
                recv_sem=r3_sem,
                device_id=(c, peer),
                device_id_type=MESH,
            ).start()

    place = x * (1 - core) + z * core
    wait_bytes(rows_all.at[place], r3_sem)
    for d in ring:
        to = (z * n + at(x, d)) * (1 - core) + (at(z, d) * n + x) * core
        pltpu.make_async_remote_copy(
            src_ref=rows_all.at[place],
            dst_ref=rows_all.at[place],
            send_sem=s4_sem,
            recv_sem=r4_sem,
            device_id=(to, g),
            device_id_type=MESH,
        ).start()
    wait_bytes(rows_all.at[pl.ds(0, n - 1)], r4_sem)
    for s in range(n):
        for group in range(2 * n):
            col = (group * n + s) * vdim
            out_ref[:, col : col + vdim] = rows_all[s, group]

    wait_bytes(q_send.at[:, pl.ds(0, 2 * n - 1)], qs_sem)
    for e in range(2):
        wait_bytes(o1_recv.at[e], s1_sem.at[e, 0])
        wait_bytes(l1_recv.at[e], s1_sem.at[e, 1])
        wait_bytes(o2_recv.at[e], s2_sem.at[e, 0])
        wait_bytes(l2_recv.at[e], s2_sem.at[e, 1])

        @pl.when(selves[e])
        def _(e=e):
            wait_bytes(rows_all.at[0, pl.ds(0, n - 1)], s3_sem.at[e])

        @pl.when(jnp.logical_not(selves[e]))
        def _(e=e):
            wait_bytes(rows_all.at[0, pl.ds(0, n)], s3_sem.at[e])

    wait_bytes(rows_all.at[pl.ds(0, n - 1)], s4_sem)


def body(n, qn, qr, lat, rk, ak, ev, ids, counts):
    tok = qn.shape[0]
    half = n * tok
    nope, rope = ak.shape[1], rk.shape[0]
    keys, latent = lat.shape
    vdim = ev.shape[2]
    pairs = n // 2
    vmem = pltpu.VMEM
    dma = pltpu.SemaphoreType.DMA
    return pl.pallas_call(
        functools.partial(kernel, n),
        out_shape=jax.ShapeDtypeStruct((tok, 2 * n * n * vdim), BF16),
        in_specs=[pl.BlockSpec(memory_space=pltpu.HBM)] * 6
        + [pl.BlockSpec(memory_space=pltpu.VMEM), pl.BlockSpec(memory_space=pltpu.SMEM)],
        out_specs=pl.BlockSpec(memory_space=pltpu.VMEM),
        scratch_shapes=[
            vmem(qn.shape, BF16),
            vmem(qr.shape, BF16),
            vmem(lat.shape, BF16),
            vmem(rk.shape, BF16),
            vmem(ak.shape, BF16),
            vmem(ev.shape, BF16),
            vmem((2, 2 * rope, keys), BF16),
            vmem((n, keys, 2 * vdim), BF16),
            vmem((n, 2, keys), F32),
            vmem((pairs, 2 * n, tok, 2 * (nope + rope)), BF16),
            vmem((pairs, 2 * half, 2 * (nope + rope)), BF16),
            vmem((2, n, half, vdim), BF16),
            vmem((2, n, 8, half), F32),
            vmem((2, n - 1, half, vdim), BF16),
            vmem((2, n - 1, 8, half), F32),
            vmem((2, half, vdim), BF16),
            vmem((2, half, BLOCK), F32),
            vmem((2, n - 1, tok, vdim), BF16),
            vmem((2, n - 1, tok, BLOCK), F32),
            vmem((2, tok, vdim), BF16),
            vmem((n, 2 * n, tok, vdim), BF16),
            dma((6,)),
            dma,
            dma((pairs,)),
            dma((2, 2)),
            dma((2, 2)),
            dma((2, 2)),
            dma((2, 2)),
            dma((2,)),
            dma,
            dma,
            dma,
        ],
        compiler_params=pltpu.CompilerParams(
            collective_id=0, has_side_effects=True, vmem_limit_bytes=60 * 1024 * 1024
        ),
        cost_estimate=pl.CostEstimate(
            flops=3 * 10**9, bytes_accessed=4 * 10**6, transcendentals=10**6
        ),
    )(qn, qr, lat, rk, ak, ev, ids, counts.T)


def solution(mesh):
    n = math.isqrt(mesh.shape["ctx"])
    return jax.shard_map(
        functools.partial(body, n),
        mesh=mesh,
        in_specs=(
            P("head", None),
            P("head", None),
            P("ctx", None),
            P(None, "ctx"),
            P("head", None, None),
            P("head", None, None),
            P("head", None, None),
            P("head", None),
        ),
        out_specs=P("head", None),
        check_vma=False,
    )
```

time: 552 us -> 73.8 us (0.13)
  blocking collectives: 313 us -> 0 us
  waiting for transfers between devices: 169 us -> 0 us
  Pallas kernels: 0 us -> 71.3 us
  starting transfers between devices: 21.7 us -> 0 us
  local copies, waits for them, and re-layouts: 17.5 us -> 1.87 us
  between operations: 14.2 us -> 0.01 us
  matrix products: 12.8 us -> 0 us
    reduce_scatter x1 -> x0, waiting for transfers between devices: 148 us -> none  [body(): lax.psum_scatter(latent_sum * factor[..., None], 'ctx', scatter_dimension...]
    pmax x1 -> x0, blocking collectives: 122 us -> none  [body(): row_top = lax.pmax(top_rows, 'ctx')]
    unnamed x1 -> x0, blocking collectives: 113 us -> none
    pallas_call x0 -> x1, Pallas kernels: none -> 71.3 us  [body(): pl.pallas_call(functools.partial(kernel, n), out_shape=jax.ShapeDtypeStru...]
    all_to_all x1 -> x0, blocking collectives: 41.5 us -> none  [body(): lax.all_to_all(merged, 'head', split_axis=0, concat_axis=1, tiled=True)]
    all_gather x1 -> x0, blocking collectives: 35.9 us -> none  [body(): merged = lax.all_gather(rows_done, 'ctx', axis=0, tiled=True)]
    all_to_all x2 -> x0, starting transfers between devices: 21.6 us -> none  [the longest x1 17.5 us: body(): lax.all_to_all(query_rope, 'head', split_axis=1, concat_axis=0, tiled=True)]
    all_to_all x2 -> x0, waiting for transfers between devices: 21.2 us -> none  [the longest x1 11.2 us: body(): lax.all_to_all(query_nope, 'head', split_axis=1, concat_axis=0, tiled=True)]
  transfers between devices with their start and end apart: 3 -> 0, of which waited for: 3 -> 0; matrix products, arithmetic and copies ran while one was open for 2% -> 0% of each run, Pallas kernels for 0% -> 0%
where the time goes in v1:
time: 73.8 us; the launch traced here: 73.2 us
  Pallas kernels  71.3 us (97%)
  local copies, waits for them, and re-layouts  1.87 us (3%)
    pallas_call x1, Pallas kernels, body(): pl.pallas_call(functools.partial(kernel, n), out_shape=jax.ShapeDtypeStru...  71.3 us
    unnamed x1, local copies, waits for them, and re-layouts  1.87 us

profile of v1, /device:TPU:1, one launch (start us, length us, event | category | flops | bytes accessed | tf_op | source)
XLA Modules:
  0.0 73.2 jit_solution(14842386565075795239)
XLA Ops:
  0.0 71.3 %shard_map.82 = bf16[16,16384]{1,0:T(8,128)(2,1)} custom-call(bf16[16,16384]{1,0:T(8,128)(2,1)} %qn_hbm.1, bf16[16,8192]{1,0:T(8,128)(2,1)} %qr_hbm.1, bf16[512,512]{1,0:T(8,128)(2,1)} %lat_hbm.1, bf16[64,512]{1,0:T(8,128)(2,1)} %rk_hbm.1, bf16[8,128,512]{2,1,0:T(8,128)(2,1)} %ak_hbm.1, bf16[8,512,128]{2,1,0:T(8,128)(2,1)} %ev_hbm.1, s32[8,2,16]{2,1,0:T(2,128)} %ids_ref.1, ...), custom_call_target="tpu_custom_call" | custom-call | flops 3000000000 | bytes 4000000 | tf_op jit(solution)/shard_map/pallas_call | solution.py:378
  71.3 1.9 %copy.10 = bf16[16,16384]{1,0:T(8,128)(2,1)} copy(bf16[16,16384]{1,0:T(8,128)(2,1)} %shard_map.82) | data formatting | bytes 1048576

commit v2 on v1

--- a/solution.py
+++ b/solution.py
@@ -11,6 +11,7 @@
 BLOCK = 128
 MESH = pl.DeviceIdType.MESH
 NONE = -1e30
+TRY = "y"
 F32 = jnp.float32
 BF16 = jnp.bfloat16
 
@@ -58,11 +59,15 @@
     l2_send,
     o2_recv,
     l2_recv,
+    shares,
     done,
     rows_all,
     load_sem,
     qs_sem,
     qr_sem,
+    fs_sem,
+    fr_sem,
+    ws_sem,
     s1_sem,
     r1_sem,
     s2_sem,
@@ -123,28 +128,66 @@
             at_r = (to * pairs + p) * wr
             q_send[p, to, :, 0:wn] = qn[:, at_n : at_n + wn]
             q_send[p, to, :, wn : wn + wr] = qr[:, at_r : at_r + wr]
-    first = lax.rem(x + z, n) // 2
-    my_rows = pl.multiple_of(core * half + y * tok, tok)
+    if pairs >= 4:
+        turn = lax.rem(x + z, 2)
+        over_x, over_z = lax.rem(z, 2), 2 + lax.rem(x, 2)
+        low, high = 1 - over_x, 5 - over_z
+        plan = [
+            ("y", low * (1 - turn) + high * turn),
+            ("x", over_x),
+            ("z", over_z),
+            ("y", low * turn + high * (1 - turn)),
+        ]
+    else:
+        plan = [(TRY, 0)]
 
     pl.semaphore_wait(barrier, len(y_peers) + 2 * len(ring))
 
-    def send_pair(i, carry):
-        p = lax.rem(first + i, pairs)
+    fetched = []
+    for i, (way, p) in enumerate(plan):
+        if way == "y":
+            continue
+        far = x if way == "x" else z
+        chip = at(y, n - far)
+        fetched.append((i, way, p, far))
+
+        def fetch(dc, p=p, i=i, chip=chip):
+            peer = 2 * chip + lax.rem(core + dc, 2)
+            pltpu.make_async_remote_copy(
+                src_ref=q_send.at[p, peer],
+                dst_ref=q_recv.at[p, y, core],
+                send_sem=fs_sem.at[i, dc],
+                recv_sem=fr_sem.at[i],
+                device_id=(c, peer),
+                device_id_type=MESH,
+            ).start()
+
+        fetch(1)
+
+        @pl.when(far != 0)
+        def _(fetch=fetch):
+            fetch(0)
+
+        @pl.when(far == 0)
+        def _(p=p, i=i):
+            pltpu.make_async_copy(q_send.at[p, g], q_recv.at[p, y, core], fr_sem.at[i]).start()
+
+    def send_direct(i, p):
         for d, dc in y_peers:
             peer = 2 * at(y, d) + lax.rem(core + dc, 2)
             pltpu.make_async_remote_copy(
                 src_ref=q_send.at[p, peer],
-                dst_ref=q_recv.at[p, pl.ds(my_rows, tok)],
-                send_sem=qs_sem,
-                recv_sem=qr_sem.at[p],
+                dst_ref=q_recv.at[p, y, core],
+                send_sem=qs_sem.at[i],
+                recv_sem=qr_sem.at[i],
                 device_id=(c, peer),
                 device_id_type=MESH,
             ).start()
-        return carry
-
-    lax.fori_loop(0, pairs, send_pair, 0)
-    for p in range(pairs):
-        q_recv[p, pl.ds(my_rows, tok)] = q_send[p, g]
+        q_recv[p, y, core] = q_send[p, g]
+
+    direct = [(i, p) for i, (way, p) in enumerate(plan) if way == "y"]
+    for i, p in direct[:1]:
+        send_direct(i, p)
 
     lane = lax.broadcasted_iota(jnp.int32, (1, slots), 1)
     for h in range(n):
@@ -160,6 +203,21 @@
     rkpad[...] = jnp.zeros_like(rkpad)
     rkpad[0, 0:rope] = rk[...]
     rkpad[1, rope : 2 * rope] = rk[...]
+    for i, way, p, far in fetched:
+        chip = at(y, far)
+        wait_bytes(q_recv.at[p, chip], fr_sem.at[i])
+        for d in ring:
+            to = z * n + at(x, d) if way == "x" else at(z, d) * n + x
+            pltpu.make_async_remote_copy(
+                src_ref=q_recv.at[p, chip],
+                dst_ref=q_recv.at[p, chip],
+                send_sem=ws_sem.at[i],
+                recv_sem=qr_sem.at[i],
+                device_id=(to, g),
+                device_id_type=MESH,
+            ).start()
+    for i, p in direct[1:]:
+        send_direct(i, p)
     loads[2].wait()
     loads[3].wait()
     vext[:, :, vdim:] = jnp.ones((n, keys, vext.shape[2] - vdim), BF16)
@@ -181,18 +239,30 @@
     key_pos = c * keys + late + lax.broadcasted_iota(jnp.int32, (1, keys - late), 1)
 
     def attend(i, carry):
-        p = lax.rem(first + i, pairs)
-        wait_bytes(q_recv.at[p, pl.ds(0, 2 * half - tok)], qr_sem.at[p])
+        p = 0
+        for j, (way, which) in enumerate(plan):
+            p = jnp.where(i == j, which, p)
+
+            @pl.when(i == j)
+            def _(way=way, which=which, j=j):
+                if way == "y":
+                    wait_bytes(q_send.at[which, pl.ds(0, 2 * n - 1)], qr_sem.at[j])
+                else:
+                    wait_bytes(q_recv.at[which, pl.ds(0, n - 1)], qr_sem.at[j])
+
+        queries = jnp.concatenate(
+            [q_recv[p, :, e].reshape(half, wn + wr) for e in range(2)], axis=0
+        )
         for k in range(2):
             h = 2 * p + k
             query_latent = jnp.dot(
-                q_recv[p, :, k * nope : (k + 1) * nope], ak[h], preferred_element_type=F32
+                queries[:, k * nope : (k + 1) * nope], ak[h], preferred_element_type=F32
             ).astype(BF16)
             scores = lax.dot_general(
                 query_latent, lat[...], (((1,), (1,)), ((), ())), preferred_element_type=F32
             )
             scores = scores + jnp.dot(
-                q_recv[p, :, wn : wn + wr], rkpad[k], preferred_element_type=F32
+                queries[:, wn : wn + wr], rkpad[k], preferred_element_type=F32
             )
             scores = scores * scale
             low, high = bias[h, 0:1], bias[h, 1:2]
@@ -217,7 +287,7 @@
             for e in range(2):
                 part = slice(e * half, (e + 1) * half)
                 o1_send[e, h] = mixed[part].astype(BF16)
-                l1_send[e, h] = jnp.transpose(level[part, 0:BLOCK])[0:8]
+                l1_send[e, h] = jnp.transpose(level[part, 0:BLOCK])[0:1]
                 mine = x if e == 0 else z
                 to = z * n + h if e == 0 else h * n + x
                 slot = lax.rem(h - mine + n, n) - 1
@@ -250,20 +320,17 @@
         wait_bytes(o1_recv.at[e], r1_sem.at[e, 0])
         wait_bytes(l1_recv.at[e], r1_sem.at[e, 1])
         levels = jnp.concatenate(
-            [l1_send[e, mine][0:1]] + [l1_recv[e, k][0:1] for k in range(n - 1)], axis=0
+            [l1_send[e, mine]] + [l1_recv[e, k] for k in range(n - 1)], axis=0
         )
         top = jnp.max(levels, axis=0, keepdims=True)
         share = jnp.exp(levels - top)
         whole = jnp.sum(share, axis=0, keepdims=True)
-        table = jnp.concatenate(
-            [share / whole, jnp.broadcast_to(top + jnp.log(whole), (n, half))], axis=0
-        )
-        columns = jnp.transpose(table)
+        columns = jnp.transpose(share / whole)
         mixed = columns[:, 0:1] * o1_send[e, mine].astype(F32)
         for k in range(n - 1):
             mixed = mixed + columns[:, k + 1 : k + 2] * o1_recv[e, k].astype(F32)
         o2_send[e] = mixed.astype(BF16)
-        l2_send[e] = jnp.broadcast_to(columns[:, n : n + 1], (half, BLOCK))
+        l2_send[e] = top + jnp.log(whole)
         for d in ring:
             other = at(z, d) if e == 0 else at(x, d)
             to = other * n + x if e == 0 else z * n + other
@@ -277,7 +344,7 @@
                 device_id_type=MESH,
             ).start()
             pltpu.make_async_remote_copy(
-                src_ref=l2_send.at[e, rows],
+                src_ref=l2_send.at[e],
                 dst_ref=l2_recv.at[e, d - 1],
                 send_sem=s2_sem.at[e, 1],
                 recv_sem=r2_sem.at[e, 1],
@@ -291,18 +358,18 @@
         wait_bytes(o2_recv.at[e], r2_sem.at[e, 0])
         wait_bytes(l2_recv.at[e], r2_sem.at[e, 1])
         rows = pl.ds(pl.multiple_of(pos * tok, tok), tok)
-        levels = [l2_send[e, rows]] + [l2_recv[e, k] for k in range(n - 1)]
-        top = functools.reduce(jnp.maximum, levels)
-        shares = [jnp.exp(level - top) for level in levels]
-        mixed = shares[0] * o2_send[e, rows].astype(F32)
-        whole = shares[0]
+        levels = jnp.concatenate([l2_send[e]] + [l2_recv[e, k] for k in range(n - 1)], axis=0)
+        share = jnp.exp(levels - jnp.max(levels, axis=0, keepdims=True))
+        shares[e] = jnp.transpose(share / jnp.sum(share, axis=0, keepdims=True))
+        columns = shares[e, rows]
+        mixed = columns[:, 0:1] * o2_send[e, rows].astype(F32)
         for k in range(n - 1):
-            mixed = mixed + shares[k + 1] * o2_recv[e, k].astype(F32)
-            whole = whole + shares[k + 1]
-        done[e] = (mixed / whole).astype(BF16)
+            mixed = mixed + columns[:, k + 1 : k + 2] * o2_recv[e, k].astype(F32)
+        done[e] = mixed.astype(BF16)
         place = x if e == 0 else z
         peer = 2 * pos + e
         is_self = g == peer
+        step = lax.rem(y - pos + n, n)
         selves.append(is_self)
         for d in ring:
             to = at(z, d) * n + x if e == 0 else z * n + at(x, d)
@@ -310,14 +377,14 @@
                 src_ref=done.at[e],
                 dst_ref=rows_all.at[place, g],
                 send_sem=s3_sem.at[e],
-                recv_sem=r3_sem,
+                recv_sem=r3_sem.at[step],
                 device_id=(to, peer),
                 device_id_type=MESH,
             ).start()
 
         @pl.when(is_self)
         def _(e=e, place=place):
-            pltpu.make_async_copy(done.at[e], rows_all.at[place, g], r3_sem).start()
+            pltpu.make_async_copy(done.at[e], rows_all.at[place, g], r3_sem.at[0]).start()
 
         @pl.when(jnp.logical_not(is_self))
         def _(e=e, place=place, peer=peer):
@@ -325,30 +392,42 @@
                 src_ref=done.at[e],
                 dst_ref=rows_all.at[place, g],
                 send_sem=s3_sem.at[e],
-                recv_sem=r3_sem,
+                recv_sem=r3_sem.at[step],
                 device_id=(c, peer),
                 device_id_type=MESH,
             ).start()
 
     place = x * (1 - core) + z * core
-    wait_bytes(rows_all.at[place], r3_sem)
-    for d in ring:
-        to = (z * n + at(x, d)) * (1 - core) + (at(z, d) * n + x) * core
-        pltpu.make_async_remote_copy(
-            src_ref=rows_all.at[place],
-            dst_ref=rows_all.at[place],
-            send_sem=s4_sem,
-            recv_sem=r4_sem,
-            device_id=(to, g),
-            device_id_type=MESH,
-        ).start()
+    for step in [0] + ring:
+        both = rows_all.at[place, pl.ds(2 * at(y, step), 2)]
+        wait_bytes(both, r3_sem.at[step])
+        for d in ring:
+            to = (z * n + at(x, d)) * (1 - core) + (at(z, d) * n + x) * core
+            pltpu.make_async_remote_copy(
+                src_ref=both,
+                dst_ref=both,
+                send_sem=s4_sem,
+                recv_sem=r4_sem,
+                device_id=(to, g),
+                device_id_type=MESH,
+            ).start()
     wait_bytes(rows_all.at[pl.ds(0, n - 1)], r4_sem)
     for s in range(n):
         for group in range(2 * n):
             col = (group * n + s) * vdim
             out_ref[:, col : col + vdim] = rows_all[s, group]
 
-    wait_bytes(q_send.at[:, pl.ds(0, 2 * n - 1)], qs_sem)
+    for i, (way, p) in enumerate(plan):
+        if way == "y":
+            wait_bytes(q_send.at[p, pl.ds(0, 2 * n - 1)], qs_sem.at[i])
+            continue
+        wait_bytes(q_send.at[p, 0], fs_sem.at[i, 1])
+
+        @pl.when((x if way == "x" else z) != 0)
+        def _(p=p, i=i):
+            wait_bytes(q_send.at[p, 0], fs_sem.at[i, 0])
+
+        wait_bytes(q_recv.at[p, pl.ds(0, n - 1)], ws_sem.at[i])
     for e in range(2):
         wait_bytes(o1_recv.at[e], s1_sem.at[e, 0])
         wait_bytes(l1_recv.at[e], s1_sem.at[e, 1])
@@ -392,26 +471,30 @@
             vmem((n, keys, 2 * vdim), BF16),
             vmem((n, 2, keys), F32),
             vmem((pairs, 2 * n, tok, 2 * (nope + rope)), BF16),
-            vmem((pairs, 2 * half, 2 * (nope + rope)), BF16),
+            vmem((pairs, n, 2, tok, 2 * (nope + rope)), BF16),
             vmem((2, n, half, vdim), BF16),
-            vmem((2, n, 8, half), F32),
+            vmem((2, n, 1, half), F32),
             vmem((2, n - 1, half, vdim), BF16),
-            vmem((2, n - 1, 8, half), F32),
+            vmem((2, n - 1, 1, half), F32),
             vmem((2, half, vdim), BF16),
-            vmem((2, half, BLOCK), F32),
+            vmem((2, 1, half), F32),
             vmem((2, n - 1, tok, vdim), BF16),
-            vmem((2, n - 1, tok, BLOCK), F32),
+            vmem((2, n - 1, 1, half), F32),
+            vmem((2, half, n), F32),
             vmem((2, tok, vdim), BF16),
             vmem((n, 2 * n, tok, vdim), BF16),
             dma((6,)),
-            dma,
+            dma((pairs,)),
+            dma((pairs,)),
+            dma((pairs, 2)),
+            dma((pairs,)),
             dma((pairs,)),
             dma((2, 2)),
             dma((2, 2)),
             dma((2, 2)),
             dma((2, 2)),
             dma((2,)),
-            dma,
+            dma((n,)),
             dma,
             dma,
         ],

time: 73.8 us -> 67.7 us (0.917)
  Pallas kernels: 71.3 us -> 65.6 us
    pallas_call x1, Pallas kernels: 71.3 us -> 65.6 us  [body(): pl.pallas_call(functools.partial(kernel, n), out_shape=jax.ShapeDtypeStru...]
where the time goes in v2:
time: 67.7 us; the launch traced here: 67.5 us
  Pallas kernels  65.6 us (97%)
  local copies, waits for them, and re-layouts  1.87 us (3%)
    pallas_call x1, Pallas kernels, body(): pl.pallas_call(functools.partial(kernel, n), out_shape=jax.ShapeDtypeStru...  65.6 us
    unnamed x1, local copies, waits for them, and re-layouts  1.87 us

profile of v2, /device:TPU:1, one launch (start us, length us, event | category | flops | bytes accessed | tf_op | source)
XLA Modules:
  0.0 67.5 jit_solution(15664493637981548883)
XLA Ops:
  0.0 65.6 %shard_map.82 = bf16[16,16384]{1,0:T(8,128)(2,1)} custom-call(bf16[16,16384]{1,0:T(8,128)(2,1)} %qn_hbm.1, bf16[16,8192]{1,0:T(8,128)(2,1)} %qr_hbm.1, bf16[512,512]{1,0:T(8,128)(2,1)} %lat_hbm.1, bf16[64,512]{1,0:T(8,128)(2,1)} %rk_hbm.1, bf16[8,128,512]{2,1,0:T(8,128)(2,1)} %ak_hbm.1, bf16[8,512,128]{2,1,0:T(8,128)(2,1)} %ev_hbm.1, s32[8,2,16]{2,1,0:T(2,128)} %ids_ref.1, ...), custom_call_target="tpu_custom_call" | custom-call | flops 3000000000 | bytes 4000000 | tf_op jit(solution)/shard_map/pallas_call | solution.py:457
  65.6 1.9 %copy.10 = bf16[16,16384]{1,0:T(8,128)(2,1)} copy(bf16[16,16384]{1,0:T(8,128)(2,1)} %shard_map.82) | data formatting | bytes 1048576

commit v3 on v2

--- a/solution.py
+++ b/solution.py
@@ -37,8 +37,8 @@
     rk_hbm,
     ak_hbm,
     ev_hbm,
-    ids_ref,
-    counts_ref,
+    ids_hbm,
+    counts_hbm,
     out_ref,
     qn,
     qr,
@@ -46,6 +46,8 @@
     rk,
     ak,
     ev,
+    ids_ref,
+    counts_ref,
     rkpad,
     vext,
     bias,
@@ -102,6 +104,8 @@
                 (ev_hbm, ev),
                 (rk_hbm, rk),
                 (ak_hbm, ak),
+                (ids_hbm, ids_ref),
+                (counts_hbm, counts_ref),
             )
         )
     ]
@@ -189,6 +193,8 @@
     for i, p in direct[:1]:
         send_direct(i, p)
 
+    loads[6].wait()
+    loads[7].wait()
     lane = lax.broadcasted_iota(jnp.int32, (1, slots), 1)
     for h in range(n):
         for q in range(2):
@@ -371,20 +377,21 @@
         is_self = g == peer
         step = lax.rem(y - pos + n, n)
         selves.append(is_self)
-        for d in ring:
-            to = at(z, d) * n + x if e == 0 else z * n + at(x, d)
-            pltpu.make_async_remote_copy(
-                src_ref=done.at[e],
-                dst_ref=rows_all.at[place, g],
-                send_sem=s3_sem.at[e],
-                recv_sem=r3_sem.at[step],
-                device_id=(to, peer),
-                device_id_type=MESH,
-            ).start()
+        for hop, shift in enumerate((0, n // 2)):
+            for d in [0] * hop + ring:
+                to = at(z, d) * n + at(x, shift) if e == 0 else at(z, shift) * n + at(x, d)
+                pltpu.make_async_remote_copy(
+                    src_ref=done.at[e],
+                    dst_ref=rows_all.at[place, g],
+                    send_sem=s3_sem.at[e],
+                    recv_sem=r3_sem.at[hop, step],
+                    device_id=(to, peer),
+                    device_id_type=MESH,
+                ).start()
 
         @pl.when(is_self)
         def _(e=e, place=place):
-            pltpu.make_async_copy(done.at[e], rows_all.at[place, g], r3_sem.at[0]).start()
+            pltpu.make_async_copy(done.at[e], rows_all.at[place, g], r3_sem.at[0, 0]).start()
 
         @pl.when(jnp.logical_not(is_self))
         def _(e=e, place=place, peer=peer):
@@ -392,30 +399,36 @@
                 src_ref=done.at[e],
                 dst_ref=rows_all.at[place, g],
                 send_sem=s3_sem.at[e],
-                recv_sem=r3_sem.at[step],
+                recv_sem=r3_sem.at[0, step],
                 device_id=(c, peer),
                 device_id_type=MESH,
             ).start()
 
     place = x * (1 - core) + z * core
-    for step in [0] + ring:
-        both = rows_all.at[place, pl.ds(2 * at(y, step), 2)]
-        wait_bytes(both, r3_sem.at[step])
-        for d in ring:
-            to = (z * n + at(x, d)) * (1 - core) + (at(z, d) * n + x) * core
-            pltpu.make_async_remote_copy(
-                src_ref=both,
-                dst_ref=both,
-                send_sem=s4_sem,
-                recv_sem=r4_sem,
-                device_id=(to, g),
-                device_id_type=MESH,
-            ).start()
-    wait_bytes(rows_all.at[pl.ds(0, n - 1)], r4_sem)
-    for s in range(n):
+    near = [d for d in ring if min(d, n - d) <= n // 4]
+    nearest = [d for d in ring if min(d, n - d) < n // 4]
+    for hop, reach in ((0, near), (1, nearest)):
+        held = at(place, hop * (n // 2))
+        for step in [0] + ring:
+            both = rows_all.at[held, pl.ds(2 * at(y, step), 2)]
+            wait_bytes(both, r3_sem.at[hop, step])
+            for d in reach:
+                to = (z * n + at(x, d)) * (1 - core) + (at(z, d) * n + x) * core
+                pltpu.make_async_remote_copy(
+                    src_ref=both,
+                    dst_ref=both,
+                    send_sem=s4_sem,
+                    recv_sem=r4_sem.at[(hop * (n // 2) - d) % n],
+                    device_id=(to, g),
+                    device_id_type=MESH,
+                ).start()
+    for off in [0, n // 2] + [d for d in ring if d != n // 2]:
+        held = at(place, off)
+        if off % (n // 2):
+            wait_bytes(rows_all.at[held], r4_sem.at[off])
         for group in range(2 * n):
-            col = (group * n + s) * vdim
-            out_ref[:, col : col + vdim] = rows_all[s, group]
+            col = pl.multiple_of((group * n + held) * vdim, vdim)
+            out_ref[:, pl.ds(col, vdim)] = rows_all[held, group]
 
     for i, (way, p) in enumerate(plan):
         if way == "y":
@@ -436,13 +449,14 @@
 
         @pl.when(selves[e])
         def _(e=e):
-            wait_bytes(rows_all.at[0, pl.ds(0, n - 1)], s3_sem.at[e])
+            wait_bytes(rows_all.at[0, pl.ds(0, 2 * n - 1)], s3_sem.at[e])
 
         @pl.when(jnp.logical_not(selves[e]))
         def _(e=e):
-            wait_bytes(rows_all.at[0, pl.ds(0, n)], s3_sem.at[e])
-
-    wait_bytes(rows_all.at[pl.ds(0, n - 1)], s4_sem)
+            wait_bytes(rows_all.at[0], s3_sem.at[e])
+
+    if near:
+        wait_bytes(rows_all.at[pl.ds(0, len(near) + len(nearest))], s4_sem)
 
 
 def body(n, qn, qr, lat, rk, ak, ev, ids, counts):
@@ -456,9 +470,8 @@
     dma = pltpu.SemaphoreType.DMA
     return pl.pallas_call(
         functools.partial(kernel, n),
-        out_shape=jax.ShapeDtypeStruct((tok, 2 * n * n * vdim), BF16),
-        in_specs=[pl.BlockSpec(memory_space=pltpu.HBM)] * 6
-        + [pl.BlockSpec(memory_space=pltpu.VMEM), pl.BlockSpec(memory_space=pltpu.SMEM)],
+        out_shape=pltpu.VMEM((tok, 2 * n * n * vdim), BF16),
+        in_specs=[pl.BlockSpec(memory_space=pltpu.HBM)] * 8,
         out_specs=pl.BlockSpec(memory_space=pltpu.VMEM),
         scratch_shapes=[
             vmem(qn.shape, BF16),
@@ -467,6 +480,8 @@
             vmem(rk.shape, BF16),
             vmem(ak.shape, BF16),
             vmem(ev.shape, BF16),
+            vmem(ids.shape, jnp.int32),
+            pltpu.SMEM(counts.shape[::-1], jnp.int32),
             vmem((2, 2 * rope, keys), BF16),
             vmem((n, keys, 2 * vdim), BF16),
             vmem((n, 2, keys), F32),
@@ -483,7 +498,7 @@
             vmem((2, half, n), F32),
             vmem((2, tok, vdim), BF16),
             vmem((n, 2 * n, tok, vdim), BF16),
-            dma((6,)),
+            dma((8,)),
             dma((pairs,)),
             dma((pairs,)),
             dma((pairs, 2)),
@@ -494,9 +509,9 @@
             dma((2, 2)),
             dma((2, 2)),
             dma((2,)),
+            dma((2, n)),
+            dma,
             dma((n,)),
-            dma,
-            dma,
         ],
         compiler_params=pltpu.CompilerParams(
             collective_id=0, has_side_effects=True, vmem_limit_bytes=60 * 1024 * 1024

time: 67.7 us -> 65.2 us (0.963)
  Pallas kernels: 65.6 us -> 64.2 us
  local copies, waits for them, and re-layouts: 1.87 us -> 0.8 us
    pallas_call x1, Pallas kernels: 65.6 us -> 64.2 us  [body(): pl.pallas_call(functools.partial(kernel, n), out_shape=pltpu.VMEM((tok, 2...]
    unnamed x1, local copies, waits for them, and re-layouts: 1.87 us -> 0.8 us
where the time goes in v3:
time: 65.2 us; the launch traced here: 65 us
  Pallas kernels  64.2 us (98%)
  local copies, waits for them, and re-layouts  0.8 us (1%)
    pallas_call x1, Pallas kernels, body(): pl.pallas_call(functools.partial(kernel, n), out_shape=pltpu.VMEM((tok, 2...  64.2 us

profile of v3, /device:TPU:1, one launch (start us, length us, event | category | flops | bytes accessed | tf_op | source)
XLA Modules:
  0.0 65.0 jit_solution(6423239447192419513)
XLA Ops:
  0.0 64.2 %shard_map.82 = bf16[16,16384]{1,0:T(8,128)(2,1)S(1)} custom-call(bf16[16,16384]{1,0:T(8,128)(2,1)} %qn_hbm.1, bf16[16,8192]{1,0:T(8,128)(2,1)} %qr_hbm.1, bf16[512,512]{1,0:T(8,128)(2,1)} %lat_hbm.1, bf16[64,512]{1,0:T(8,128)(2,1)} %rk_hbm.1, bf16[8,128,512]{2,1,0:T(8,128)(2,1)} %ak_hbm.1, bf16[8,512,128]{2,1,0:T(8,128)(2,1)} %ev_hbm.1, ...), custom_call_target="tpu_custom_call" | custom-call | flops 3000000000 | bytes 4000000 | tf_op jit(solution)/shard_map/pallas_call | solution.py:471
  64.2 0.8 %copy.10 = bf16[16,16384]{1,0:T(8,128)(2,1)} copy(bf16[16,16384]{1,0:T(8,128)(2,1)S(1)} %shard_map.82) | data formatting | bytes 1048576

commit v4 on v3

--- a/solution.py
+++ b/solution.py
@@ -93,6 +93,8 @@
     pairs = n // 2
     wn, wr = 2 * nope, 2 * rope
     ring = ring_order(n)
+    near = [d for d in ring if min(d, n - d) <= n // 4]
+    nearest = [d for d in ring if min(d, n - d) < n // 4]
 
     loads = [
         pltpu.make_async_copy(src, dst, load_sem.at[i])
@@ -152,29 +154,30 @@
         if way == "y":
             continue
         far = x if way == "x" else z
-        chip = at(y, n - far)
         fetched.append((i, way, p, far))
-
-        def fetch(dc, p=p, i=i, chip=chip):
-            peer = 2 * chip + lax.rem(core + dc, 2)
-            pltpu.make_async_remote_copy(
-                src_ref=q_send.at[p, peer],
-                dst_ref=q_recv.at[p, y, core],
-                send_sem=fs_sem.at[i, dc],
-                recv_sem=fr_sem.at[i],
-                device_id=(c, peer),
-                device_id_type=MESH,
-            ).start()
-
-        fetch(1)
-
-        @pl.when(far != 0)
-        def _(fetch=fetch):
-            fetch(0)
-
-        @pl.when(far == 0)
-        def _(p=p, i=i):
-            pltpu.make_async_copy(q_send.at[p, g], q_recv.at[p, y, core], fr_sem.at[i]).start()
+        for hop in range(2):
+            chip = at(y, 2 * n - far - hop * (n // 2))
+
+            def fetch(dc, p=p, i=i, hop=hop, chip=chip):
+                peer = 2 * chip + lax.rem(core + dc, 2)
+                pltpu.make_async_remote_copy(
+                    src_ref=q_send.at[p, peer],
+                    dst_ref=q_recv.at[p, y, core],
+                    send_sem=fs_sem.at[i, hop, dc],
+                    recv_sem=fr_sem.at[i, hop],
+                    device_id=(c, peer),
+                    device_id_type=MESH,
+                ).start()
+
+            fetch(1)
+
+            @pl.when(far != hop * (n // 2))
+            def _(fetch=fetch):
+                fetch(0)
+
+            @pl.when(far == hop * (n // 2))
+            def _(p=p, i=i, hop=hop):
+                pltpu.make_async_copy(q_send.at[p, g], q_recv.at[p, y, core], fr_sem.at[i, hop]).start()
 
     def send_direct(i, p):
         for d, dc in y_peers:
@@ -210,18 +213,19 @@
     rkpad[0, 0:rope] = rk[...]
     rkpad[1, rope : 2 * rope] = rk[...]
     for i, way, p, far in fetched:
-        chip = at(y, far)
-        wait_bytes(q_recv.at[p, chip], fr_sem.at[i])
-        for d in ring:
-            to = z * n + at(x, d) if way == "x" else at(z, d) * n + x
-            pltpu.make_async_remote_copy(
-                src_ref=q_recv.at[p, chip],
-                dst_ref=q_recv.at[p, chip],
-                send_sem=ws_sem.at[i],
-                recv_sem=qr_sem.at[i],
-                device_id=(to, g),
-                device_id_type=MESH,
-            ).start()
+        for hop, reach in ((0, near), (1, nearest)):
+            chip = at(y, far + hop * (n // 2))
+            wait_bytes(q_recv.at[p, chip], fr_sem.at[i, hop])
+            for d in reach:
+                to = z * n + at(x, d) if way == "x" else at(z, d) * n + x
+                pltpu.make_async_remote_copy(
+                    src_ref=q_recv.at[p, chip],
+                    dst_ref=q_recv.at[p, chip],
+                    send_sem=ws_sem.at[i],
+                    recv_sem=qr_sem.at[i],
+                    device_id=(to, g),
+                    device_id_type=MESH,
+                ).start()
     for i, p in direct[1:]:
         send_direct(i, p)
     loads[2].wait()
@@ -253,8 +257,8 @@
             def _(way=way, which=which, j=j):
                 if way == "y":
                     wait_bytes(q_send.at[which, pl.ds(0, 2 * n - 1)], qr_sem.at[j])
-                else:
-                    wait_bytes(q_recv.at[which, pl.ds(0, n - 1)], qr_sem.at[j])
+                elif near:
+                    wait_bytes(q_recv.at[which, pl.ds(0, n - 2)], qr_sem.at[j])
 
         queries = jnp.concatenate(
             [q_recv[p, :, e].reshape(half, wn + wr) for e in range(2)], axis=0
@@ -405,8 +409,6 @@
             ).start()
 
     place = x * (1 - core) + z * core
-    near = [d for d in ring if min(d, n - d) <= n // 4]
-    nearest = [d for d in ring if min(d, n - d) < n // 4]
     for hop, reach in ((0, near), (1, nearest)):
         held = at(place, hop * (n // 2))
         for step in [0] + ring:
@@ -434,13 +436,15 @@
         if way == "y":
             wait_bytes(q_send.at[p, pl.ds(0, 2 * n - 1)], qs_sem.at[i])
             continue
-        wait_bytes(q_send.at[p, 0], fs_sem.at[i, 1])
-
-        @pl.when((x if way == "x" else z) != 0)
-        def _(p=p, i=i):
-            wait_bytes(q_send.at[p, 0], fs_sem.at[i, 0])
-
-        wait_bytes(q_recv.at[p, pl.ds(0, n - 1)], ws_sem.at[i])
+        for hop in range(2):
+            wait_bytes(q_send.at[p, 0], fs_sem.at[i, hop, 1])
+
+            @pl.when((x if way == "x" else z) != hop * (n // 2))
+            def _(p=p, i=i, hop=hop):
+                wait_bytes(q_send.at[p, 0], fs_sem.at[i, hop, 0])
+
+        if near:
+            wait_bytes(q_recv.at[p, pl.ds(0, n - 2)], ws_sem.at[i])
     for e in range(2):
         wait_bytes(o1_recv.at[e], s1_sem.at[e, 0])
         wait_bytes(l1_recv.at[e], s1_sem.at[e, 1])
@@ -501,8 +505,8 @@
             dma((8,)),
             dma((pairs,)),
             dma((pairs,)),
+            dma((pairs, 2, 2)),
             dma((pairs, 2)),
-            dma((pairs,)),
             dma((pairs,)),
             dma((2, 2)),
             dma((2, 2)),

time: 65.2 us -> 65.1 us (level)
  no operation moved by 1% of the time
where the time goes in v4:
time: 65.1 us; the launch traced here: 65 us
  Pallas kernels  64.2 us (99%)
  local copies, waits for them, and re-layouts  0.8 us (1%)
    pallas_call x1, Pallas kernels, body(): pl.pallas_call(functools.partial(kernel, n), out_shape=pltpu.VMEM((tok, 2...  64.2 us

profile of v4, /device:TPU:1, one launch (start us, length us, event | category | flops | bytes accessed | tf_op | source)
XLA Modules:
  0.0 65.0 jit_solution(13610878815821669173)
XLA Ops:
  0.0 64.2 %shard_map.82 = bf16[16,16384]{1,0:T(8,128)(2,1)S(1)} custom-call(bf16[16,16384]{1,0:T(8,128)(2,1)} %qn_hbm.1, bf16[16,8192]{1,0:T(8,128)(2,1)} %qr_hbm.1, bf16[512,512]{1,0:T(8,128)(2,1)} %lat_hbm.1, bf16[64,512]{1,0:T(8,128)(2,1)} %rk_hbm.1, bf16[8,128,512]{2,1,0:T(8,128)(2,1)} %ak_hbm.1, bf16[8,512,128]{2,1,0:T(8,128)(2,1)} %ev_hbm.1, ...), custom_call_target="tpu_custom_call" | custom-call | flops 3000000000 | bytes 4000000 | tf_op jit(solution)/shard_map/pallas_call | solution.py:475
  64.2 0.8 %copy.10 = bf16[16,16384]{1,0:T(8,128)(2,1)} copy(bf16[16,16384]{1,0:T(8,128)(2,1)S(1)} %shard_map.82) | data formatting | bytes 1048576

commit v5 on v4

--- a/solution.py
+++ b/solution.py
@@ -226,8 +226,9 @@
                     device_id=(to, g),
                     device_id_type=MESH,
                 ).start()
-    for i, p in direct[1:]:
-        send_direct(i, p)
+        if way == "x":
+            for j, other in direct[1:]:
+                send_direct(j, other)
     loads[2].wait()
     loads[3].wait()
     vext[:, :, vdim:] = jnp.ones((n, keys, vext.shape[2] - vdim), BF16)

time: 65.1 us -> 65.4 us (level)
  no operation moved by 1% of the time
where the time goes in v5:
time: 65.4 us; the launch traced here: 65.2 us
  Pallas kernels  64.4 us (98%)
  local copies, waits for them, and re-layouts  0.8 us (1%)
    pallas_call x1, Pallas kernels, body(): pl.pallas_call(functools.partial(kernel, n), out_shape=pltpu.VMEM((tok, 2...  64.4 us

profile of v5, /device:TPU:1, one launch (start us, length us, event | category | flops | bytes accessed | tf_op | source)
XLA Modules:
  0.0 65.2 jit_solution(10657243163955265251)
XLA Ops:
  0.0 64.4 %shard_map.82 = bf16[16,16384]{1,0:T(8,128)(2,1)S(1)} custom-call(bf16[16,16384]{1,0:T(8,128)(2,1)} %qn_hbm.1, bf16[16,8192]{1,0:T(8,128)(2,1)} %qr_hbm.1, bf16[512,512]{1,0:T(8,128)(2,1)} %lat_hbm.1, bf16[64,512]{1,0:T(8,128)(2,1)} %rk_hbm.1, bf16[8,128,512]{2,1,0:T(8,128)(2,1)} %ak_hbm.1, bf16[8,512,128]{2,1,0:T(8,128)(2,1)} %ev_hbm.1, ...), custom_call_target="tpu_custom_call" | custom-call | flops 3000000000 | bytes 4000000 | tf_op jit(solution)/shard_map/pallas_call | solution.py:476
  64.4 0.8 %copy.10 = bf16[16,16384]{1,0:T(8,128)(2,1)} copy(bf16[16,16384]{1,0:T(8,128)(2,1)S(1)} %shard_map.82) | data formatting | bytes 1048576
